TPU v7x, 512 devices: a whole 4x4x16 slice. The times are simulated.
512 devices in a mesh: dp: 8 (over x, core), expouter: 8 (over z_lo), expinner: 8 (over z_hi, y).
Axes of the slice: x: 4, y: 4, z: 16 (z_hi: 2, z_lo: 8; z = z_hi * 8 + z_lo), core: 2. Of those that a mesh axis runs over, the one named last changes fastest.
Arguments:
- tokens: bfloat16 [65536, 1024], P(('dp', 'expouter', 'expinner')), may hold values from -6 to 6
- cotangent: bfloat16 [65536, 1024], P(('dp', 'expouter', 'expinner')), may hold values from -6 to 6
- gate_probs: float32 [65536, 2], P(('dp', 'expouter', 'expinner')), may hold values from 0.05 to 1
- expert_ids: int32 [65536, 2], P(('dp', 'expouter', 'expinner')), may hold values from 0 to 63, all different within a row; in each aligned block of 128 rows (0 to 127, 128 to 255, ...) at most 5 rows name the same one
- gate_weight: bfloat16 [64, 1024, 768], P(('expouter', 'expinner'), 'dp'), may hold values from -0.1875 to 0.1875
- up_weight: bfloat16 [64, 1024, 768], P(('expouter', 'expinner'), 'dp'), may hold values from -0.1875 to 0.1875
- down_weight: bfloat16 [64, 1024, 768], P(('expouter', 'expinner'), 'dp'), may hold values from -0.21875 to 0.21875
Outputs:
- mixed: bfloat16 [65536, 1024], P(('dp', 'expouter', 'expinner'))
- grad_tokens: bfloat16 [65536, 1024], P(('dp', 'expouter', 'expinner'))
- grad_probs: float32 [65536, 2], P(('dp', 'expouter', 'expinner'))
- grad_gate: float32 [64, 1024, 768], P(('expouter', 'expinner'), 'dp')
- grad_up: float32 [64, 1024, 768], P(('expouter', 'expinner'), 'dp')
- grad_down: float32 [64, 1024, 768], P(('expouter', 'expinner'), 'dp')
Inputs may be any that keep to these rules, and one draw needn't show every extreme that they name: `expert_ids`: among the tokens of one device (aligned blocks of 128 tokens) no expert is named more than 5 times, a bound that some block reaches; a token's 2 experts differ.
All inputs are finite; a program needn't handle non-finite values.
Results may differ from a plain program's by a relative error of at most 0.0065.
Values may be sent and summed in bfloat16 or wider, within the bound.
A program may use at most 64 MiB of HBM per device.

v0:
```python
import jax
import jax.numpy as jnp
from jax import lax
from jax.sharding import PartitionSpec as P


def expert_pass(rows_x, rows_o, gate_mat, up_mat, down_mat):
    pre_gate = jnp.dot(rows_x, gate_mat, preferred_element_type=jnp.float32)
    pre_up = jnp.dot(rows_x, up_mat, preferred_element_type=jnp.float32)
    sigma = jax.nn.sigmoid(pre_gate)
    active = pre_gate * sigma
    hidden = (active * pre_up).astype(jnp.bfloat16)
    expert_out = jnp.dot(hidden, down_mat.T, preferred_element_type=jnp.float32).astype(
        jnp.bfloat16
    )
    grad_hidden = jnp.dot(rows_o, down_mat, preferred_element_type=jnp.float32)
    slope = sigma * (1.0 + pre_gate * (1.0 - sigma))
    grad_gate_pre = (grad_hidden * pre_up * slope).astype(jnp.bfloat16)
    grad_up_pre = (grad_hidden * active).astype(jnp.bfloat16)
    grad_rows = (
        jnp.dot(grad_gate_pre, gate_mat.T, preferred_element_type=jnp.float32)
        + jnp.dot(grad_up_pre, up_mat.T, preferred_element_type=jnp.float32)
    ).astype(jnp.bfloat16)
    return (hidden, expert_out, grad_gate_pre, grad_up_pre, grad_rows)


def contract_rows(left, right):
    return lax.dot_general(
        left, right, (((0,), (0,)), ((), ())), preferred_element_type=jnp.float32
    )


def per_device(tokens, cotangent, gate_probs, expert_ids, gate_weight, up_weight, down_weight):
    tok_rows, model_width = tokens.shape
    top_count = expert_ids.shape[1]
    outer_count = lax.axis_size("expouter")
    inner_count = lax.axis_size("expinner")
    expert_count = outer_count * inner_count
    capacity = max(2, tok_rows * top_count * 5 // (4 * expert_count))
    slots_all = expert_count * capacity
    assigns = tok_rows * top_count
    flat_route = expert_ids.reshape(assigns)
    order = jnp.arange(assigns, dtype=jnp.int32)
    before = (order[None, :] < order[:, None]) & (flat_route[None, :] == flat_route[:, None])
    slot_pos = jnp.sum(before.astype(jnp.int32), axis=1)
    target = flat_route * capacity + slot_pos
    select = (target[None, :] == jnp.arange(slots_all, dtype=jnp.int32)[:, None]).astype(
        jnp.bfloat16
    )
    token_select = select.reshape(slots_all, tok_rows, top_count).sum(axis=2)
    send_x = jnp.dot(token_select, tokens, preferred_element_type=jnp.float32).astype(jnp.bfloat16)
    scaled = (gate_probs[:, :, None] * cotangent[:, None, :].astype(jnp.float32)).astype(
        jnp.bfloat16
    )
    send_o = jnp.dot(
        select, scaled.reshape(assigns, model_width), preferred_element_type=jnp.float32
    ).astype(jnp.bfloat16)
    weights_all = (
        lax.all_gather(gate_weight, "dp", axis=1, tiled=True),
        lax.all_gather(up_weight, "dp", axis=1, tiled=True),
        lax.all_gather(down_weight, "dp", axis=1, tiled=True),
    )
    gate_full = weights_all[0][0]
    up_full = weights_all[1][0]
    down_full = weights_all[2][0]
    shaped = (
        send_x.reshape(expert_count, capacity, model_width),
        send_o.reshape(expert_count, capacity, model_width),
    )
    recv_x, recv_o = (
        lax.all_to_all(
            shaped[0], ("expouter", "expinner"), split_axis=0, concat_axis=0, tiled=True
        ),
        lax.all_to_all(
            shaped[1], ("expouter", "expinner"), split_axis=0, concat_axis=0, tiled=True
        ),
    )
    rows_x = recv_x.reshape(slots_all, model_width)
    rows_o = recv_o.reshape(slots_all, model_width)
    hidden, expert_out, grad_gate_pre, grad_up_pre, grad_rows = expert_pass(
        rows_x, rows_o, gate_full, up_full, down_full
    )
    returned = (
        expert_out.reshape(expert_count, capacity, model_width),
        grad_rows.reshape(expert_count, capacity, model_width),
    )
    back_out, back_grad = (
        lax.all_to_all(
            returned[0], ("expouter", "expinner"), split_axis=0, concat_axis=0, tiled=True
        ),
        lax.all_to_all(
            returned[1], ("expouter", "expinner"), split_axis=0, concat_axis=0, tiled=True
        ),
    )
    pick_out = back_out.reshape(slots_all, model_width)[target].reshape(
        tok_rows, top_count, model_width
    )
    pick_grad = back_grad.reshape(slots_all, model_width)[target].reshape(
        tok_rows, top_count, model_width
    )
    pick_float = pick_out.astype(jnp.float32)
    mixed = jnp.sum(gate_probs[:, :, None] * pick_float, axis=1).astype(jnp.bfloat16)
    grad_tokens = jnp.sum(pick_grad.astype(jnp.float32), axis=1).astype(jnp.bfloat16)
    grad_probs = jnp.sum(cotangent[:, None, :].astype(jnp.float32) * pick_float, axis=2)
    cols_x, cols_o = (
        lax.all_to_all(rows_x, "dp", split_axis=1, concat_axis=0, tiled=True),
        lax.all_to_all(rows_o, "dp", split_axis=1, concat_axis=0, tiled=True),
    )
    grad_g = contract_rows(cols_x, lax.all_gather(grad_gate_pre, "dp", axis=0, tiled=True))
    grad_u = contract_rows(cols_x, lax.all_gather(grad_up_pre, "dp", axis=0, tiled=True))
    grad_d = contract_rows(cols_o, lax.all_gather(hidden, "dp", axis=0, tiled=True))
    return (mixed, grad_tokens, grad_probs, grad_g[None], grad_u[None], grad_d[None])


def solution(mesh):
    return jax.shard_map(
        per_device,
        mesh=mesh,
        in_specs=(
            P(("dp", "expouter", "expinner"), None),
            P(("dp", "expouter", "expinner"), None),
            P(("dp", "expouter", "expinner"), None),
            P(("dp", "expouter", "expinner"), None),
            P(("expouter", "expinner"), "dp", None),
            P(("expouter", "expinner"), "dp", None),
            P(("expouter", "expinner"), "dp", None),
        ),
        out_specs=(
            P(("dp", "expouter", "expinner"), None),
            P(("dp", "expouter", "expinner"), None),
            P(("dp", "expouter", "expinner"), None),
            P(("expouter", "expinner"), "dp", None),
            P(("expouter", "expinner"), "dp", None),
            P(("expouter", "expinner"), "dp", None),
        ),
        check_vma=False,
    )
```

profile of v0, /device:TPU:1, one launch (start us, length us, event | category | flops | bytes accessed | tf_op | source)
XLA Modules:
  0.0 329.3 jit_solution(1604184112315230597)
XLA Ops:
  7.2 0.0 all-gather.9.cloned.1.call-start
  7.2 0.7 all-gather.9.cloned.1.call-update
  7.9 0.8 copy.29
  8.7 0.1 eq.35
  8.8 0.2 convert_reduce_fusion
  9.0 0.1 reduce_sum.56
  9.2 0.1 copy.31
  9.3 0.1 fusion.25
  9.3 0.3 convolution_convert_fusion
  9.7 1.2 reshape.115
  10.9 19.4 %all-to-all-start = ((bf16[64,5,1024]{2,1,0:T(8,128)(2,1)}), bf16[64,5,1024]{2,1,0:T(8,128)(2,1)S(1)}, u32[]{:S(2)}, u32[]{:S(2)}) async-start(bf16[64,5,1024]{2,1,0:T(8,128)(2,1)} %reshape.115), calls=%async_computation | async-start | bytes 2097152 | tf_op jit(solution)/shard_map/all_to_all | solution.py:71
  30.3 0.0 all-gather.11.cloned.1.call-start
  30.4 0.7 all-gather.11.cloned.1.call-update
  31.1 0.1 copy.28
  31.2 0.1 mul.91
  31.3 0.3 mul.93
  31.6 0.7 mul.94
  32.4 0.4 convolution_convert_fusion.1
  32.8 1.2 reshape.119
  34.0 48.6 %all-to-all-done = bf16[64,5,1024]{2,1,0:T(8,128)(2,1)S(1)} async-done(((bf16[64,5,1024]{2,1,0:T(8,128)(2,1)}), bf16[64,5,1024]{2,1,0:T(8,128)(2,1)S(1)}, u32[]{:S(2)}, u32[]{:S(2)}) %all-to-all-start) | async-done | bytes 655392 | tf_op jit(solution)/shard_map/all_to_all | solution.py:71
  82.6 8.4 %all-to-all-start.2 = ((bf16[64,5,1024]{2,1,0:T(8,128)(2,1)}), bf16[64,5,1024]{2,1,0:T(8,128)(2,1)S(1)}, u32[]{:S(2)}, u32[]{:S(2)}) async-start(bf16[64,5,1024]{2,1,0:T(8,128)(2,1)} %reshape.119), calls=%async_computation.2 | async-start | bytes 2097152 | tf_op jit(solution)/shard_map/all_to_all | solution.py:74
  91.0 0.0 all-gather.7.cloned.1.call-start
  91.1 0.7 all-gather.7.cloned.1.call-update
  91.8 0.0 all-gather.13.cloned.1.call-start
  91.8 0.3 reshape.116
  92.1 51.8 %all-to-all-done.2 = bf16[64,5,1024]{2,1,0:T(8,128)(2,1)S(1)} async-done(((bf16[64,5,1024]{2,1,0:T(8,128)(2,1)}), bf16[64,5,1024]{2,1,0:T(8,128)(2,1)S(1)}, u32[]{:S(2)}, u32[]{:S(2)}) %all-to-all-start.2) | async-done | bytes 655392 | tf_op jit(solution)/shard_map/all_to_all | solution.py:74
  143.9 1.1 reshape.120
  145.0 3.0 fusion.6
  148.0 3.3 fusion
  151.3 4.1 %multiply_convert_fusion.2 = (bf16[320,768]{1,0:T(8,128)(2,1)}, bf16[320,768]{1,0:T(8,128)(2,1)}, bf16[320,768]{1,0:T(8,128)(2,1)}) fusion(f32[320,768]{1,0:T(8,128)} %fusion, f32[320,768]{1,0:T(8,128)} %fusion.6, bf16[320,1024]{1,0:T(8,128)(2,1)S(1)} %reshape.116, bf16[1,1024,768]{2,1,0:T(8,128)(2,1)} %all-gather.7.cloned.1.call-done), kind=kOutput, calls=%fused_computation.26 | convolution fusion | flops 507002880 | bytes 5668864 | tf_op jit(solution)/shard_map/dot_general | solution.py:8
  155.4 0.0 all-gather.15.cloned.1.call-start
  155.4 0.5 all-gather.15.cloned.1.call-update
  156.0 0.0 all-gather.17.cloned.1.call-start
  156.0 0.5 all-gather.17.cloned.1.call-update
  156.6 2.2 fusion.4
  158.9 0.7 fusion.18
  159.6 1.3 reshape.121
  160.8 7.4 %all-to-all-start.3 = ((bf16[64,5,1024]{2,1,0:T(8,128)(2,1)}), bf16[64,5,1024]{2,1,0:T(8,128)(2,1)S(1)}, u32[]{:S(2)}, u32[]{:S(2)}) async-start(bf16[64,5,1024]{2,1,0:T(8,128)(2,1)} %reshape.121), calls=%async_computation.3 | async-start | bytes 2097152 | tf_op jit(solution)/shard_map/all_to_all | solution.py:91
  168.2 3.1 fusion.15
  171.4 2.1 reshape.117
  173.5 47.7 %all-to-all-done.3 = bf16[64,5,1024]{2,1,0:T(8,128)(2,1)S(1)} async-done(((bf16[64,5,1024]{2,1,0:T(8,128)(2,1)}), bf16[64,5,1024]{2,1,0:T(8,128)(2,1)S(1)}, u32[]{:S(2)}, u32[]{:S(2)}) %all-to-all-start.3) | async-done | bytes 655392 | tf_op jit(solution)/shard_map/all_to_all | solution.py:91
  221.2 7.4 %all-to-all-start.1 = ((bf16[64,5,1024]{2,1,0:T(8,128)(2,1)}), bf16[64,5,1024]{2,1,0:T(8,128)(2,1)}, u32[]{:S(2)}, u32[]{:S(2)}) async-start(bf16[64,5,1024]{2,1,0:T(8,128)(2,1)} %reshape.117), calls=%async_computation.1 | async-start | bytes 2097152 | tf_op jit(solution)/shard_map/all_to_all | solution.py:88
  228.6 1.8 convert_element_type.62
  230.4 0.1 mul.87
  230.5 1.6 all_to_all.44
  232.1 2.0 copy.33
  234.2 46.0 %all-to-all-done.1 = bf16[64,5,1024]{2,1,0:T(8,128)(2,1)} async-done(((bf16[64,5,1024]{2,1,0:T(8,128)(2,1)}), bf16[64,5,1024]{2,1,0:T(8,128)(2,1)}, u32[]{:S(2)}, u32[]{:S(2)}) %all-to-all-start.1) | async-done | bytes 655392 | tf_op jit(solution)/shard_map/all_to_all | solution.py:88
  280.1 8.1 %all-to-all-start.4 = ((bf16[320,8,128]{2,0,1:T(8,128)(2,1)}), bf16[320,8,128]{2,0,1:T(8,128)(2,1)S(1)}, u32[]{:S(2)}, u32[]{:S(2)}) async-start(bf16[320,8,128]{2,0,1:T(8,128)(2,1)} %copy.33), calls=%async_computation.4 | async-start | bytes 1310720 | tf_op jit(solution)/shard_map/all_to_all | solution.py:106
  288.3 1.6 all_to_all.48
  289.9 2.0 copy.34
  291.9 0.3 reshape.122
  292.2 1.2 gather_fusion.1
  293.4 0.2 reshape.123
  293.6 1.4 reshape.118
  295.0 1.2 gather_fusion
  296.2 0.7 reshape.124
  296.8 3.6 %multiply_reduce_fusion = (f32[128,2]{1,0:T(8,128)S(1)}, bf16[128,1024]{1,0:T(8,128)(2,1)}) fusion(f32[128,2,1024]{2,1,0:T(2,128)S(1)} %reshape.124, f32[128,1024]{1,0:T(8,128)} %convert_element_type.62, f32[128,2]{1,0:T(8,128)S(1)} %copy.28), kind=kLoop, calls=%fused_computation.22 | loop fusion | flops 917248 | bytes 1837056 | tf_op jit(solution)/shard_map/reduce_sum | solution.py:104
  300.4 0.6 copy.35
  301.1 2.1 reduce_sum.60
  303.2 4.8 %all-to-all-start.5 = ((bf16[320,8,128]{2,0,1:T(8,128)(2,1)}), bf16[320,8,128]{2,0,1:T(8,128)(2,1)S(1)}, u32[]{:S(2)}, u32[]{:S(2)}) async-start(bf16[320,8,128]{2,0,1:T(8,128)(2,1)} %copy.34), calls=%async_computation.5 | async-start | bytes 1310720 | tf_op jit(solution)/shard_map/all_to_all | solution.py:107
  308.0 3.6 %convolution_bitcast_fusion.2 = f32[1,128,768]{2,1,0:T(8,128)} fusion(bf16[2560,128]{1,0:T(8,128)(2,1)S(1)} %bitcast.51, bf16[2560,768]{1,0:T(8,128)(2,1)} %all-gather.13.cloned.1.call-done), kind=kOutput, calls=%fused_computation.21 | convolution fusion | flops 503316480 | bytes 4980736 | tf_op jit(solution)/shard_map/dot_general | solution.py:28
  311.6 3.6 %convolution_bitcast_fusion.1 = f32[1,128,768]{2,1,0:T(8,128)} fusion(bf16[2560,128]{1,0:T(8,128)(2,1)S(1)} %bitcast.52, bf16[2560,768]{1,0:T(8,128)(2,1)} %all-gather.15.cloned.1.call-done), kind=kOutput, calls=%fused_computation.20 | convolution fusion | flops 503316480 | bytes 4980736 | tf_op jit(solution)/shard_map/dot_general | solution.py:28
  315.2 3.7 %all-to-all-done.5 = bf16[320,8,128]{2,0,1:T(8,128)(2,1)S(1)} async-done(((bf16[320,8,128]{2,0,1:T(8,128)(2,1)}), bf16[320,8,128]{2,0,1:T(8,128)(2,1)S(1)}, u32[]{:S(2)}, u32[]{:S(2)}) %all-to-all-start.5) | async-done | bytes 655392 | tf_op jit(solution)/shard_map/all_to_all | solution.py:107
  318.9 3.6 %convolution_bitcast_fusion = f32[1,128,768]{2,1,0:T(8,128)} fusion(bf16[2560,128]{1,0:T(8,128)(2,1)S(1)} %bitcast.53, bf16[2560,768]{1,0:T(8,128)(2,1)} %all-gather.17.cloned.1.call-done), kind=kOutput, calls=%fused_computation.19 | convolution fusion | flops 503316480 | bytes 4980736 | tf_op jit(solution)/shard_map/dot_general | solution.py:28
  (24 shorter events, 0.1 us)
Async XLA Ops:
  7.2 2.2 copy-start
  7.2 137.8 %all-gather.9.cloned.1.call-start = ((), (), s32[]{:S(2)}) async-start(), calls=%async_computation.7 | async-start | bytes 1769472 | tf_op jit(solution)/shard_map/all_gather | solution.py:60
  10.9 20.2 %copy-start.5 = (f32[128,2]{0,1:T(2,128)S(1)}, f32[128,2]{0,1:T(2,128)}, u32[]{:S(2)}) copy-start(f32[128,2]{0,1:T(2,128)} %param.9) | copy-start | bytes 3076
  10.9 20.4 %copy-start.4 = (bf16[128,1024]{1,0:T(8,128)(2,1)S(1)}, bf16[128,1024]{1,0:T(8,128)(2,1)}, u32[]{:S(2)}) copy-start(bf16[128,1024]{1,0:T(8,128)(2,1)} %param.8) | copy-start | bytes 786436
  10.9 71.8 %all-to-all-start = ((bf16[64,5,1024]{2,1,0:T(8,128)(2,1)}), bf16[64,5,1024]{2,1,0:T(8,128)(2,1)S(1)}, u32[]{:S(2)}, u32[]{:S(2)}) async-start(bf16[64,5,1024]{2,1,0:T(8,128)(2,1)} %reshape.115), calls=%async_computation | async-start | bytes 2097152 | tf_op jit(solution)/shard_map/all_to_all | solution.py:71
  30.3 117.7 %all-gather.11.cloned.1.call-start = ((), (), s32[]{:S(2)}) async-start(), calls=%async_computation.8 | async-start | bytes 1769472 | tf_op jit(solution)/shard_map/all_gather | solution.py:61
  82.6 61.2 %all-to-all-start.2 = ((bf16[64,5,1024]{2,1,0:T(8,128)(2,1)}), bf16[64,5,1024]{2,1,0:T(8,128)(2,1)S(1)}, u32[]{:S(2)}, u32[]{:S(2)}) async-start(bf16[64,5,1024]{2,1,0:T(8,128)(2,1)} %reshape.119), calls=%async_computation.2 | async-start | bytes 2097152 | tf_op jit(solution)/shard_map/all_to_all | solution.py:74
  91.0 60.3 %all-gather.7.cloned.1.call-start = ((), (), s32[]{:S(2)}) async-start(), calls=%async_computation.6 | async-start | bytes 1769472 | tf_op jit(solution)/shard_map/all_gather | solution.py:59
  91.8 216.2 %all-gather.13.cloned.1.call-start = ((), (), s32[]{:S(2)}) async-start(), calls=%async_computation.9 | async-start | bytes 4423680 | tf_op jit(solution)/shard_map/all_gather | solution.py:109
  155.4 1.2 copy-start.1
  155.4 156.2 %all-gather.15.cloned.1.call-start = ((), (), s32[]{:S(2)}) async-start(), calls=%async_computation.10 | async-start | bytes 4423680 | tf_op jit(solution)/shard_map/all_gather | solution.py:110
  156.0 162.9 %all-gather.17.cloned.1.call-start = ((), (), s32[]{:S(2)}) async-start(), calls=%async_computation.11 | async-start | bytes 4423680 | tf_op jit(solution)/shard_map/all_gather | solution.py:111
  156.6 2.3 copy-start.2
  156.6 2.3 copy-start.3
  160.8 60.4 %all-to-all-start.3 = ((bf16[64,5,1024]{2,1,0:T(8,128)(2,1)}), bf16[64,5,1024]{2,1,0:T(8,128)(2,1)S(1)}, u32[]{:S(2)}, u32[]{:S(2)}) async-start(bf16[64,5,1024]{2,1,0:T(8,128)(2,1)} %reshape.121), calls=%async_computation.3 | async-start | bytes 2097152 | tf_op jit(solution)/shard_map/all_to_all | solution.py:91
  221.2 58.9 %all-to-all-start.1 = ((bf16[64,5,1024]{2,1,0:T(8,128)(2,1)}), bf16[64,5,1024]{2,1,0:T(8,128)(2,1)}, u32[]{:S(2)}, u32[]{:S(2)}) async-start(bf16[64,5,1024]{2,1,0:T(8,128)(2,1)} %reshape.117), calls=%async_computation.1 | async-start | bytes 2097152 | tf_op jit(solution)/shard_map/all_to_all | solution.py:88
  280.1 23.0 %all-to-all-start.4 = ((bf16[320,8,128]{2,0,1:T(8,128)(2,1)}), bf16[320,8,128]{2,0,1:T(8,128)(2,1)S(1)}, u32[]{:S(2)}, u32[]{:S(2)}) async-start(bf16[320,8,128]{2,0,1:T(8,128)(2,1)} %copy.33), calls=%async_computation.4 | async-start | bytes 1310720 | tf_op jit(solution)/shard_map/all_to_all | solution.py:106
  303.2 15.7 %all-to-all-start.5 = ((bf16[320,8,128]{2,0,1:T(8,128)(2,1)}), bf16[320,8,128]{2,0,1:T(8,128)(2,1)S(1)}, u32[]{:S(2)}, u32[]{:S(2)}) async-start(bf16[320,8,128]{2,0,1:T(8,128)(2,1)} %copy.34), calls=%async_computation.5 | async-start | bytes 1310720 | tf_op jit(solution)/shard_map/all_to_all | solution.py:107
Sparse Core Ops, SparseCore 0:
  10.1 37.8 all-gather.8
  50.2 32.1 all-gather.10
  94.0 33.9 all-gather.6
  155.5 33.2 all-gather.12
  190.8 38.6 all-gather.14
  231.5 38.6 all-gather.16
where the time goes:
time: 330 us; the launch traced here: 329 us
  waiting for transfers between devices  201 us (61%)
  starting transfers between devices  55.7 us (17%)
  matrix products  28 us (8%)
  local copies, waits for them, and re-layouts  22.6 us (7%)
  between operations  14.4 us (4%)
  other arithmetic  7.8 us (2%)
    all_to_all x1, waiting for transfers between devices, per_device(): lax.all_to_all(shaped[1], ('expouter', 'expinner'), split_axis=0, concat_...  51.8 us
    all_to_all x1, waiting for transfers between devices, per_device(): lax.all_to_all(shaped[0], ('expouter', 'expinner'), split_axis=0, concat_...  48.6 us
    all_to_all x1, waiting for transfers between devices, per_device(): lax.all_to_all(returned[1], ('expouter', 'expinner'), split_axis=0, conca...  47.7 us
    all_to_all x1, waiting for transfers between devices, per_device(): lax.all_to_all(returned[0], ('expouter', 'expinner'), split_axis=0, conca...  46 us
    all_to_all x1, starting transfers between devices, per_device(): lax.all_to_all(shaped[0], ('expouter', 'expinner'), split_axis=0, concat_...  19.4 us
    dot_general x3, matrix products, contract_rows(): lax.dot_general(left, right, (((0,), (0,)), ((), ())), preferred_element_...  10.8 us
    all_to_all x1, starting transfers between devices, per_device(): lax.all_to_all(shaped[1], ('expouter', 'expinner'), split_axis=0, concat_...  8.38 us
    all_to_all x1, starting transfers between devices, per_device(): lax.all_to_all(rows_x, 'dp', split_axis=1, concat_axis=0, tiled=True)  8.13 us
  transfers between devices with their start and end apart: 12, of which 5 were waited for; matrix products, arithmetic and copies ran while one was open for 14% of the time, Pallas kernels for 0%

commit v1 on v0

--- a/solution.py
+++ b/solution.py
@@ -2,6 +2,22 @@
 import jax.numpy as jnp
 from jax import lax
 from jax.sharding import PartitionSpec as P
+
+
+def swapped_with_each(value, axis, split, join):
+    ways, here = (lax.axis_size(axis), lax.axis_index(axis))
+    width = value.shape[split] // ways
+    shape = list(value.shape)
+    shape[split] = width
+    height = shape[join]
+    shape[join] = height * ways
+    full = jnp.zeros(shape, value.dtype)
+    for mask in range(ways):
+        part = lax.dynamic_slice_in_dim(value, (here ^ mask) * width, width, axis=split)
+        if mask:
+            part = lax.ppermute(part, axis, [(d, d ^ mask) for d in range(ways)])
+        full = lax.dynamic_update_slice_in_dim(full, part, (here ^ mask) * height, axis=join)
+    return full
 
 
 def expert_pass(rows_x, rows_o, gate_mat, up_mat, down_mat):
@@ -103,7 +119,7 @@
     grad_tokens = jnp.sum(pick_grad.astype(jnp.float32), axis=1).astype(jnp.bfloat16)
     grad_probs = jnp.sum(cotangent[:, None, :].astype(jnp.float32) * pick_float, axis=2)
     cols_x, cols_o = (
-        lax.all_to_all(rows_x, "dp", split_axis=1, concat_axis=0, tiled=True),
+        swapped_with_each(rows_x, "dp", 1, 0),
         lax.all_to_all(rows_o, "dp", split_axis=1, concat_axis=0, tiled=True),
     )
     grad_g = contract_rows(cols_x, lax.all_gather(grad_gate_pre, "dp", axis=0, tiled=True))

time: 330 us -> 315 us (0.955)
  waiting for transfers between devices: 201 us -> 167 us
  starting transfers between devices: 55.7 us -> 74 us
    all_to_all x1, waiting for transfers between devices: 47.7 us -> 10.8 us  [per_device(): lax.all_to_all(returned[1], ('expouter', 'expinner'), split_axis=0, conca...]
    ppermute x0 -> x7, starting transfers between devices: none -> 23.4 us  [swapped_with_each(): part = lax.ppermute(part, axis, [(d, d ^ mask) for d in range(ways)])]
    all_to_all x1, starting transfers between devices: 19.4 us -> 8.28 us  [per_device(): lax.all_to_all(shaped[0], ('expouter', 'expinner'), split_axis=0, concat_...]
    all_to_all x1, starting transfers between devices: 8.38 us -> 19.3 us  [per_device(): lax.all_to_all(shaped[1], ('expouter', 'expinner'), split_axis=0, concat_...]
    all_to_all x1 -> x0, starting transfers between devices: 8.13 us -> none  [per_device(): lax.all_to_all(rows_x, 'dp', split_axis=1, concat_axis=0, tiled=True)]
    dynamic_update_slice x0 -> x7, local copies, waits for them, and re-layouts: none -> 4.56 us  [swapped_with_each(): lax.dynamic_update_slice_in_dim(full, part, (here ^ mask) * height, axis=...]
    ppermute x0 -> x7, waiting for transfers between devices: none -> 3.93 us  [swapped_with_each(): part = lax.ppermute(part, axis, [(d, d ^ mask) for d in range(ways)])]
    all_to_all x1, waiting for transfers between devices: 3.7 us -> 0.01 us  [per_device(): lax.all_to_all(rows_o, 'dp', split_axis=1, concat_axis=0, tiled=True)]
  transfers between devices with their start and end apart: 12 -> 18, of which waited for: 5 -> 5; matrix products, arithmetic and copies ran while one was open for 14% -> 16% of each run, Pallas kernels for 0% -> 0%
where the time goes in v1:
time: 315 us; the launch traced here: 314 us
  waiting for transfers between devices  167 us (53%)
  starting transfers between devices  74 us (23%)
  matrix products  26.5 us (8%)
  local copies, waits for them, and re-layouts  25 us (8%)
  between operations  14.7 us (5%)
  other arithmetic  6.61 us (2%)
    all_to_all x1, waiting for transfers between devices, per_device(): lax.all_to_all(shaped[0], ('expouter', 'expinner'), split_axis=0, concat_...  51 us
    all_to_all x1, waiting for transfers between devices, per_device(): lax.all_to_all(shaped[1], ('expouter', 'expinner'), split_axis=0, concat_...  49.7 us
    all_to_all x1, waiting for transfers between devices, per_device(): lax.all_to_all(returned[0], ('expouter', 'expinner'), split_axis=0, conca...  48.3 us
    ppermute x7, starting transfers between devices, swapped_with_each(): part = lax.ppermute(part, axis, [(d, d ^ mask) for d in range(ways)])  23.4 us
    all_to_all x1, starting transfers between devices, per_device(): lax.all_to_all(shaped[1], ('expouter', 'expinner'), split_axis=0, concat_...  19.3 us
    dot_general x3, matrix products, contract_rows(): lax.dot_general(left, right, (((0,), (0,)), ((), ())), preferred_element_...  11 us
    all_to_all x1, waiting for transfers between devices, per_device(): lax.all_to_all(returned[1], ('expouter', 'expinner'), split_axis=0, conca...  10.8 us
    all_to_all x1, starting transfers between devices, per_device(): lax.all_to_all(shaped[0], ('expouter', 'expinner'), split_axis=0, concat_...  8.28 us
  transfers between devices with their start and end apart: 18, of which 5 were waited for; matrix products, arithmetic and copies ran while one was open for 16% of the time, Pallas kernels for 0%

profile of v1, /device:TPU:1, one launch (start us, length us, event | category | flops | bytes accessed | tf_op | source)
XLA Modules:
  0.0 313.7 jit_solution(13512445272144939882)
XLA Ops:
  7.2 0.7 all-gather.11.cloned.1.call-update
  7.9 1.2 mul.141
  9.2 0.7 mul.142
  10.0 0.1 mul.139
  10.3 0.1 eq.35
  10.4 0.2 convert_reduce_fusion
  10.7 0.4 convolution_convert_fusion.1
  11.1 1.2 reshape.115
  12.3 19.3 %all-to-all-start.2 = ((bf16[64,5,1024]{2,1,0:T(8,128)(2,1)}), bf16[64,5,1024]{2,1,0:T(8,128)(2,1)S(1)}, u32[]{:S(2)}, u32[]{:S(2)}) async-start(bf16[64,5,1024]{2,1,0:T(8,128)(2,1)} %reshape.115), calls=%async_computation.2 | async-start | bytes 2097152 | tf_op jit(solution)/shard_map/all_to_all | solution.py:90
  31.6 0.7 all-gather.9.cloned.1.call-update
  32.4 0.1 reduce_sum.56
  32.7 0.3 convolution_convert_fusion
  33.0 1.2 reshape.111
  34.2 49.7 %all-to-all-done.2 = bf16[64,5,1024]{2,1,0:T(8,128)(2,1)S(1)} async-done(((bf16[64,5,1024]{2,1,0:T(8,128)(2,1)}), bf16[64,5,1024]{2,1,0:T(8,128)(2,1)S(1)}, u32[]{:S(2)}, u32[]{:S(2)}) %all-to-all-start.2) | async-done | bytes 655392 | tf_op jit(solution)/shard_map/all_to_all | solution.py:90
  83.9 8.3 %all-to-all-start = ((bf16[64,5,1024]{2,1,0:T(8,128)(2,1)}), bf16[64,5,1024]{2,1,0:T(8,128)(2,1)S(1)}, u32[]{:S(2)}, u32[]{:S(2)}) async-start(bf16[64,5,1024]{2,1,0:T(8,128)(2,1)} %reshape.111), calls=%async_computation | async-start | bytes 2097152 | tf_op jit(solution)/shard_map/all_to_all | solution.py:87
  92.3 0.7 all-gather.7.cloned.1.call-update
  93.0 1.1 reshape.116
  94.1 51.0 %all-to-all-done = bf16[64,5,1024]{2,1,0:T(8,128)(2,1)S(1)} async-done(((bf16[64,5,1024]{2,1,0:T(8,128)(2,1)}), bf16[64,5,1024]{2,1,0:T(8,128)(2,1)S(1)}, u32[]{:S(2)}, u32[]{:S(2)}) %all-to-all-start) | async-done | bytes 655392 | tf_op jit(solution)/shard_map/all_to_all | solution.py:87
  145.1 0.3 reshape.112
  145.4 2.5 fusion
  147.9 3.0 fusion.6
  150.9 3.8 %multiply_convert_fusion.2 = (bf16[320,768]{1,0:T(8,128)(2,1)}, bf16[320,768]{1,0:T(8,128)(2,1)}, bf16[320,768]{1,0:T(8,128)(2,1)}) fusion(f32[320,768]{1,0:T(8,128)S(1)} %fusion, f32[320,768]{1,0:T(8,128)} %fusion.6, bf16[320,1024]{1,0:T(8,128)(2,1)S(1)} %reshape.112, bf16[1,1024,768]{2,1,0:T(8,128)(2,1)} %all-gather.7.cloned.1.call-done), kind=kOutput, calls=%fused_computation.26 | convolution fusion | flops 507002880 | bytes 5668864 | tf_op jit(solution)/shard_map/dot_general | solution.py:24
  154.8 0.5 all-gather.15.cloned.1.call-update
  155.4 0.5 all-gather.17.cloned.1.call-update
  155.9 2.3 fusion.15
  158.2 1.2 reshape.113
  159.4 7.4 %all-to-all-start.1 = ((bf16[64,5,1024]{2,1,0:T(8,128)(2,1)}), bf16[64,5,1024]{2,1,0:T(8,128)(2,1)S(1)}, u32[]{:S(2)}, u32[]{:S(2)}) async-start(bf16[64,5,1024]{2,1,0:T(8,128)(2,1)} %reshape.113), calls=%async_computation.1 | async-start | bytes 2097152 | tf_op jit(solution)/shard_map/all_to_all | solution.py:104
  166.8 2.6 fusion.4
  169.4 0.7 fusion.18
  170.1 1.2 reshape.117
  171.4 48.3 %all-to-all-done.1 = bf16[64,5,1024]{2,1,0:T(8,128)(2,1)S(1)} async-done(((bf16[64,5,1024]{2,1,0:T(8,128)(2,1)}), bf16[64,5,1024]{2,1,0:T(8,128)(2,1)S(1)}, u32[]{:S(2)}, u32[]{:S(2)}) %all-to-all-start.1) | async-done | bytes 655392 | tf_op jit(solution)/shard_map/all_to_all | solution.py:104
  219.7 7.3 %all-to-all-start.3 = ((bf16[64,5,1024]{2,1,0:T(8,128)(2,1)}), bf16[64,5,1024]{2,1,0:T(8,128)(2,1)}, u32[]{:S(2)}, u32[]{:S(2)}) async-start(bf16[64,5,1024]{2,1,0:T(8,128)(2,1)} %reshape.117), calls=%async_computation.3 | async-start | bytes 2097152 | tf_op jit(solution)/shard_map/all_to_all | solution.py:107
  227.0 0.8 convert_element_type.62
  227.9 0.1 mul.135
  228.2 1.9 constant_dynamic-slice_fusion
  230.1 4.2 %collective-permute-start = (bf16[320,128]{1,0:T(8,128)(2,1)}, bf16[320,128]{1,0:T(8,128)(2,1)}, u32[]{:S(2)}, u32[]{:S(2)}) collective-permute-start(bf16[320,128]{1,0:T(8,128)(2,1)} %get-tuple-element.29), channel_id=1, source_target_pairs={{0,64},{64,0},{128,192},{192,128},{256,320},{320,256},{384,448},{4... | collective-permute-start | bytes 245768 | tf_op jit(solution)/shard_map/ppermute | solution.py:18
  234.3 3.1 collective-permute-start.1
  237.4 2.3 collective-permute-start.2
  239.8 4.6 %collective-permute-start.3 = (bf16[320,128]{1,0:T(8,128)(2,1)S(1)}, bf16[320,128]{1,0:T(8,128)(2,1)}, u32[]{:S(2)}, u32[]{:S(2)}) collective-permute-start(bf16[320,128]{1,0:T(8,128)(2,1)S(1)} %get-tuple-element.26), channel_id=1, source_target_pairs={{0,256},{64,320},{128,384},{192,448},{256,0},{320,64},{384,128},{4... | collective-permute-start | bytes 245768 | tf_op jit(solution)/shard_map/ppermute | solution.py:18
  244.4 2.5 collective-permute-start.4
  246.9 1.6 all_to_all.30
  248.6 2.2 copy.31
  250.7 4.4 %collective-permute-start.5 = (bf16[320,128]{1,0:T(8,128)(2,1)S(1)}, bf16[320,128]{1,0:T(8,128)(2,1)S(1)}, u32[]{:S(2)}, u32[]{:S(2)}) collective-permute-start(bf16[320,128]{1,0:T(8,128)(2,1)S(1)} %get-tuple-element.24), channel_id=1, source_target_pairs={{0,384},{64,448},{128,256},{192,320},{256,128},{320,192},{384,0},{... | collective-permute-start | bytes 245768 | tf_op jit(solution)/shard_map/ppermute | solution.py:18
  255.2 0.9 constant_dynamic-update-slice_fusion.5
  256.1 2.2 collective-permute-start.6
  258.2 0.9 constant_dynamic-update-slice_fusion.4
  259.2 0.9 constant_dynamic-update-slice_fusion.3
  260.1 0.9 constant_dynamic-update-slice_fusion.2
  261.0 0.9 constant_dynamic-update-slice_fusion.1
  261.9 3.9 %collective-permute-done.6 = bf16[320,128]{1,0:T(8,128)(2,1)S(1)} collective-permute-done((bf16[320,128]{1,0:T(8,128)(2,1)S(1)}, bf16[320,128]{1,0:T(8,128)(2,1)S(1)}, u32[]{:S(2)}, u32[]{:S(2)}) %collective-permute-start.6) | collective-permute-done | bytes 81952 | tf_op jit(solution)/shard_map/ppermute | solution.py:18
  265.9 0.3 reshape.114
  266.2 1.2 gather_fusion
  267.3 0.7 reshape.120
  268.0 10.8 %all-to-all-done.3 = bf16[64,5,1024]{2,1,0:T(8,128)(2,1)} async-done(((bf16[64,5,1024]{2,1,0:T(8,128)(2,1)}), bf16[64,5,1024]{2,1,0:T(8,128)(2,1)}, u32[]{:S(2)}, u32[]{:S(2)}) %all-to-all-start.3) | async-done | bytes 655392 | tf_op jit(solution)/shard_map/all_to_all | solution.py:107
  278.7 8.2 %all-to-all-start.4 = ((bf16[320,8,128]{2,0,1:T(8,128)(2,1)}), bf16[320,8,128]{2,0,1:T(8,128)(2,1)}, u32[]{:S(2)}, u32[]{:S(2)}) async-start(bf16[320,8,128]{2,0,1:T(8,128)(2,1)} %copy.31), calls=%async_computation.4 | async-start | bytes 1310720 | tf_op jit(solution)/shard_map/all_to_all | solution.py:123
  286.9 1.4 reshape.118
  288.4 1.2 gather_fusion.1
  289.5 0.2 reshape.119
  289.8 2.1 reduce_sum.60
  291.8 3.4 %multiply_reduce_fusion = (f32[128,2]{1,0:T(8,128)S(1)}, bf16[128,1024]{1,0:T(8,128)(2,1)}) fusion(f32[128,2,1024]{2,1,0:T(2,128)S(1)} %reshape.120, f32[128,1024]{1,0:T(8,128)S(1)} %copy-done.2, f32[128,2]{1,0:T(8,128)} %copy-done.7), kind=kLoop, calls=%fused_computation.22 | loop fusion | flops 917248 | bytes 1837056 | tf_op jit(solution)/shard_map/reduce_sum | solution.py:120
  295.3 0.6 copy.32
  295.9 3.6 %convolution_bitcast_fusion.2 = f32[1,128,768]{2,1,0:T(8,128)} fusion(bf16[2560,128]{1,0:T(8,128)(2,1)S(1)} %constant_dynamic-update-slice_fusion.6, bf16[2560,768]{1,0:T(8,128)(2,1)} %all-gather.13.cloned.1.call-done), kind=kOutput, calls=%fused_computation.21 | convolution fusion | flops 503316480 | bytes 4980736 | tf_op jit(solution)/shard_map/dot_general | solution.py:44
  299.5 3.6 %convolution_bitcast_fusion.1 = f32[1,128,768]{2,1,0:T(8,128)} fusion(bf16[2560,128]{1,0:T(8,128)(2,1)S(1)} %constant_dynamic-update-slice_fusion.6, bf16[2560,768]{1,0:T(8,128)(2,1)} %all-gather.15.cloned.1.call-done), kind=kOutput, calls=%fused_computation.20 | convolution fusion | flops 503316480 | bytes 4980736 | tf_op jit(solution)/shard_map/dot_general | solution.py:44
  303.1 3.8 %convolution_bitcast_fusion = f32[1,128,768]{2,1,0:T(8,128)} fusion(bf16[2560,128]{1,0:T(8,128)(2,1)} %bitcast.8, bf16[2560,768]{1,0:T(8,128)(2,1)} %all-gather.17.cloned.1.call-done), kind=kOutput, calls=%fused_computation.19 | convolution fusion | flops 503316480 | bytes 4980736 | tf_op jit(solution)/shard_map/dot_general | solution.py:44
  (51 shorter events, 0.9 us)
Async XLA Ops:
  7.2 25.5 %copy-start = (bf16[128,1024]{1,0:T(8,128)(2,1)S(1)}, bf16[128,1024]{1,0:T(8,128)(2,1)}, u32[]{:S(2)}) copy-start(bf16[128,1024]{1,0:T(8,128)(2,1)} %param.7) | copy-start | bytes 786436
  7.2 138.2 %all-gather.11.cloned.1.call-start = ((), (), s32[]{:S(2)}) async-start(), calls=%async_computation.7 | async-start | bytes 1769472 | tf_op jit(solution)/shard_map/all_gather | solution.py:77
  7.9 2.0 copy-start.8
  7.9 2.2 copy-start.9
  10.0 0.6 copy-start.7
  12.3 71.6 %all-to-all-start.2 = ((bf16[64,5,1024]{2,1,0:T(8,128)(2,1)}), bf16[64,5,1024]{2,1,0:T(8,128)(2,1)S(1)}, u32[]{:S(2)}, u32[]{:S(2)}) async-start(bf16[64,5,1024]{2,1,0:T(8,128)(2,1)} %reshape.115), calls=%async_computation.2 | async-start | bytes 2097152 | tf_op jit(solution)/shard_map/all_to_all | solution.py:90
  31.6 116.3 %all-gather.9.cloned.1.call-start = ((), (), s32[]{:S(2)}) async-start(), calls=%async_computation.6 | async-start | bytes 1769472 | tf_op jit(solution)/shard_map/all_gather | solution.py:76
  83.9 61.1 %all-to-all-start = ((bf16[64,5,1024]{2,1,0:T(8,128)(2,1)}), bf16[64,5,1024]{2,1,0:T(8,128)(2,1)S(1)}, u32[]{:S(2)}, u32[]{:S(2)}) async-start(bf16[64,5,1024]{2,1,0:T(8,128)(2,1)} %reshape.111), calls=%async_computation | async-start | bytes 2097152 | tf_op jit(solution)/shard_map/all_to_all | solution.py:87
  92.2 58.7 %all-gather.7.cloned.1.call-start = ((), (), s32[]{:S(2)}) async-start(), calls=%async_computation.5 | async-start | bytes 1769472 | tf_op jit(solution)/shard_map/all_gather | solution.py:75
  93.0 202.9 %all-gather.13.cloned.1.call-start = ((), (), s32[]{:S(2)}) async-start(), calls=%async_computation.8 | async-start | bytes 4423680 | tf_op jit(solution)/shard_map/all_gather | solution.py:125
  145.3 5.6 %copy-start.1 = (bf16[320,1024]{1,0:T(8,128)(2,1)}, bf16[320,1024]{1,0:T(8,128)(2,1)S(1)}, u32[]{:S(2)}) copy-start(bf16[320,1024]{1,0:T(8,128)(2,1)S(1)} %reshape.112) | copy-start | bytes 1966084
  154.7 144.7 %all-gather.15.cloned.1.call-start = ((), (), s32[]{:S(2)}) async-start(), calls=%async_computation.9 | async-start | bytes 4423680 | tf_op jit(solution)/shard_map/all_gather | solution.py:126
  155.3 147.7 %all-gather.17.cloned.1.call-start = ((), (), s32[]{:S(2)}) async-start(), calls=%async_computation.10 | async-start | bytes 4423680 | tf_op jit(solution)/shard_map/all_gather | solution.py:127
  158.2 8.6 %copy-start.3 = (bf16[320,768]{1,0:T(8,128)(2,1)S(1)}, bf16[320,768]{1,0:T(8,128)(2,1)}, u32[]{:S(2)}) copy-start(bf16[320,768]{1,0:T(8,128)(2,1)} %get-tuple-element.21) | copy-start | bytes 1474564
  159.4 60.3 %all-to-all-start.1 = ((bf16[64,5,1024]{2,1,0:T(8,128)(2,1)}), bf16[64,5,1024]{2,1,0:T(8,128)(2,1)S(1)}, u32[]{:S(2)}, u32[]{:S(2)}) async-start(bf16[64,5,1024]{2,1,0:T(8,128)(2,1)} %reshape.113), calls=%async_computation.1 | async-start | bytes 2097152 | tf_op jit(solution)/shard_map/all_to_all | solution.py:104
  166.8 2.6 copy-start.4
  166.8 2.6 copy-start.5
  170.1 56.9 %copy-start.6 = (bf16[128,1024]{1,0:T(8,128)(2,1)S(1)}, bf16[128,1024]{1,0:T(8,128)(2,1)}, u32[]{:S(2)}) copy-start(bf16[128,1024]{1,0:T(8,128)(2,1)} %param.8) | copy-start | bytes 786436
  219.7 59.0 %all-to-all-start.3 = ((bf16[64,5,1024]{2,1,0:T(8,128)(2,1)}), bf16[64,5,1024]{2,1,0:T(8,128)(2,1)}, u32[]{:S(2)}, u32[]{:S(2)}) async-start(bf16[64,5,1024]{2,1,0:T(8,128)(2,1)} %reshape.117), calls=%async_computation.3 | async-start | bytes 2097152 | tf_op jit(solution)/shard_map/all_to_all | solution.py:107
  230.1 20.7 %collective-permute-start = (bf16[320,128]{1,0:T(8,128)(2,1)}, bf16[320,128]{1,0:T(8,128)(2,1)}, u32[]{:S(2)}, u32[]{:S(2)}) collective-permute-start(bf16[320,128]{1,0:T(8,128)(2,1)} %get-tuple-element.29), channel_id=1, source_target_pairs={{0,64},{64,0},{128,192},{192,128},{256,320},{320,256},{384,448},{4... | collective-permute-start | bytes 245768 | tf_op jit(solution)/shard_map/ppermute | solution.py:18
  234.3 21.8 %collective-permute-start.1 = (bf16[320,128]{1,0:T(8,128)(2,1)S(1)}, bf16[320,128]{1,0:T(8,128)(2,1)}, u32[]{:S(2)}, u32[]{:S(2)}) collective-permute-start(bf16[320,128]{1,0:T(8,128)(2,1)S(1)} %get-tuple-element.28), channel_id=1, source_target_pairs={{0,128},{64,192},{128,0},{192,64},{256,384},{320,448},{384,256},{4... | collective-permute-start | bytes 245768 | tf_op jit(solution)/shard_map/ppermute | solution.py:18
  237.4 21.8 %collective-permute-start.2 = (bf16[320,128]{1,0:T(8,128)(2,1)S(1)}, bf16[320,128]{1,0:T(8,128)(2,1)}, u32[]{:S(2)}, u32[]{:S(2)}) collective-permute-start(bf16[320,128]{1,0:T(8,128)(2,1)S(1)} %get-tuple-element.27), channel_id=1, source_target_pairs={{0,192},{64,128},{128,64},{192,0},{256,448},{320,384},{384,320},{4... | collective-permute-start | bytes 245768 | tf_op jit(solution)/shard_map/ppermute | solution.py:18
  239.8 20.3 %collective-permute-start.3 = (bf16[320,128]{1,0:T(8,128)(2,1)S(1)}, bf16[320,128]{1,0:T(8,128)(2,1)}, u32[]{:S(2)}, u32[]{:S(2)}) collective-permute-start(bf16[320,128]{1,0:T(8,128)(2,1)S(1)} %get-tuple-element.26), channel_id=1, source_target_pairs={{0,256},{64,320},{128,384},{192,448},{256,0},{320,64},{384,128},{4... | collective-permute-start | bytes 245768 | tf_op jit(solution)/shard_map/ppermute | solution.py:18
  244.4 16.6 %collective-permute-start.4 = (bf16[320,128]{1,0:T(8,128)(2,1)S(1)}, bf16[320,128]{1,0:T(8,128)(2,1)}, u32[]{:S(2)}, u32[]{:S(2)}) collective-permute-start(bf16[320,128]{1,0:T(8,128)(2,1)S(1)} %get-tuple-element.25), channel_id=1, source_target_pairs={{0,320},{64,256},{128,448},{192,384},{256,64},{320,0},{384,192},{4... | collective-permute-start | bytes 245768 | tf_op jit(solution)/shard_map/ppermute | solution.py:18
  250.7 11.2 %collective-permute-start.5 = (bf16[320,128]{1,0:T(8,128)(2,1)S(1)}, bf16[320,128]{1,0:T(8,128)(2,1)S(1)}, u32[]{:S(2)}, u32[]{:S(2)}) collective-permute-start(bf16[320,128]{1,0:T(8,128)(2,1)S(1)} %get-tuple-element.24), channel_id=1, source_target_pairs={{0,384},{64,448},{128,256},{192,320},{256,128},{320,192},{384,0},{... | collective-permute-start | bytes 245768 | tf_op jit(solution)/shard_map/ppermute | solution.py:18
  256.1 9.8 %collective-permute-start.6 = (bf16[320,128]{1,0:T(8,128)(2,1)S(1)}, bf16[320,128]{1,0:T(8,128)(2,1)S(1)}, u32[]{:S(2)}, u32[]{:S(2)}) collective-permute-start(bf16[320,128]{1,0:T(8,128)(2,1)S(1)} %get-tuple-element.23), channel_id=1, source_target_pairs={{0,448},{64,384},{128,320},{192,256},{256,192},{320,128},{384,64},... | collective-permute-start | bytes 245768 | tf_op jit(solution)/shard_map/ppermute | solution.py:18
  278.7 24.3 %all-to-all-start.4 = ((bf16[320,8,128]{2,0,1:T(8,128)(2,1)}), bf16[320,8,128]{2,0,1:T(8,128)(2,1)}, u32[]{:S(2)}, u32[]{:S(2)}) async-start(bf16[320,8,128]{2,0,1:T(8,128)(2,1)} %copy.31), calls=%async_computation.4 | async-start | bytes 1310720 | tf_op jit(solution)/shard_map/all_to_all | solution.py:123
  289.5 2.3 copy-start.2
Sparse Core Ops, SparseCore 0:
  10.1 37.6 all-gather.10
  50.0 32.3 all-gather.8
  95.2 34.0 all-gather.6
  154.9 33.3 all-gather.12
  190.2 38.6 all-gather.14
  230.9 42.7 all-gather.16
